TPU v7x, 256 devices: a whole 4x4x8 slice. The times are simulated.
256 devices in a mesh: tile: 16 (over z, core), lev: 4 (over x), tag: 4 (over y).
Axes of the slice: x: 4, y: 4, z: 8, core: 2. Of those that a mesh axis runs over, the one named last changes fastest.
Arguments:
- parent_field: float32 [8, 32, 256, 1024], P('tag', 'lev', 'tile'), may hold values from -6 to 6
- nest_field: float32 [8, 32, 256, 1024], P('tag', 'lev', 'tile'), may hold values from -6 to 6
- parent_mixing: float32 [32, 256, 1024], P('lev', 'tile'), may hold values from 0.05 to 5
- parent_eastward: float32 [256, 1024], P('tile'), may hold values from 0.02 to 0.12
- parent_northward: float32 [256, 1024], P('tile'), may hold values from 0.02 to 0.12
- nest_eastward: float32 [256, 1024], P('tile'), may hold values from 0.02 to 0.12
- nest_northward: float32 [256, 1024], P('tile'), may hold values from 0.02 to 0.12
- strip_tile: int32 [16, 256], replicated, may hold values from 0 to 15, as said below
- strip_block: int32 [16, 256], replicated, may hold values from 0 to 127
- strip_target: int32 [16, 256], replicated, may hold values from 0 to 127
- strip_count: int32 [16], replicated, may hold values from 1 to 256, as said below
Outputs:
- parent_adjoint: float32 [8, 32, 256, 1024], P('tag', 'lev', 'tile')
- nest_adjoint: float32 [8, 32, 256, 1024], P('tag', 'lev', 'tile')
- bulk_adjoint: float32 [32, 256, 1024], P('lev', 'tile', 'tag')
Inputs may be any that keep to these rules, and one draw needn't show every extreme that they name: `strip_tile`: among the first strip_count[j] entries of row j, every parent tile appears at most 16 times; in the row whose count is 256 every parent tile appears exactly 16 times. `strip_count`: exactly one nest tile lists 256 strips; every other lists at most 128.
All inputs are finite; a program needn't handle non-finite values.
Results may differ from a plain program's by a relative error of at most 0.0003.
Values sent between devices are 32-bit elements; how exact they have to be, the bound alone decides.
A program may use at most 64 MiB of HBM per device.

v0:
```python
import jax
import jax.numpy as jnp
from jax import lax
from jax.sharding import PartitionSpec as P

CAP = 16
NSUB = 3
HIGHEST = lax.Precision.HIGHEST


def extended(cells, sides, width):
    for axis, dim in sides:
        count = lax.axis_size(axis)
        ends = count - 1
        head = lax.slice_in_dim(cells, 0, width, axis=dim)
        tail = lax.slice_in_dim(cells, cells.shape[dim] - width, cells.shape[dim], axis=dim)
        cells = jnp.concatenate(
            [
                lax.ppermute(tail, axis, [(i, (i + 1) % count) for i in range(ends)]),
                cells,
                lax.ppermute(head, axis, [((i + 1) % count, i) for i in range(ends)]),
            ],
            axis=dim,
        )
    return cells


def tridiagonal(source, mixing):
    level_count = mixing.shape[0]
    mixing_up = jnp.concatenate([mixing[1:], jnp.zeros_like(mixing[:1])], axis=0)
    diagonal = 1.0 + mixing + mixing_up
    ratio_now = jnp.zeros_like(mixing[0])
    carry_now = jnp.zeros_like(source[:, 0])
    ratios = []
    carries = []
    for lev_index in range(level_count):
        pivot_now = diagonal[lev_index] + mixing[lev_index] * ratio_now
        ratio_now = -mixing_up[lev_index] / pivot_now
        carry_now = (source[:, lev_index] + mixing[lev_index] * carry_now) / pivot_now
        ratios.append(ratio_now)
        carries.append(carry_now)
    value_now = carries[level_count - 1]
    results = [value_now]
    for lev_index in range(level_count - 2, -1, -1):
        value_now = carries[lev_index] - ratios[lev_index] * value_now
        results.append(value_now)
    return jnp.stack(results[::-1], axis=1)


def relax(padded, eastward):
    center = padded[:-1, 1:-1]
    row_above = padded[:-1, :-2]
    row_below = padded[:-1, 2:]
    north_here = padded[-1, 1:-1]
    north_above = padded[-1, :-2]
    zero_column = jnp.zeros_like(center[:, :, :1])
    east_cell = jnp.concatenate([center[:, :, 1:], zero_column], axis=2)
    west_cell = jnp.concatenate([zero_column, center[:, :, :-1]], axis=2)
    west_rate = jnp.concatenate([jnp.zeros_like(eastward[:, :1]), eastward[:, :-1]], axis=1)
    return (
        center
        + north_here * (row_below - center)
        + north_above * (row_above - center)
        + eastward * (east_cell - center)
        + west_rate * (west_cell - center)
    )


def rims(stacked):
    return extended(stacked, (("tile", 1),), 1)


def advance(start, solved, parent_eastward, parent_northward, nest_eastward, nest_northward):
    tag_count, level_count, row_count, col_count = start.shape
    line_count = tag_count * level_count
    nest_now = start.reshape(line_count, row_count, col_count)
    parent_now = solved.reshape(line_count, row_count, col_count)
    for sub_step in range(NSUB):
        nest_stack = jnp.concatenate([nest_now, nest_northward[None]], axis=0)
        if sub_step == 0:
            parent_stack = jnp.concatenate([parent_now, parent_northward[None]], axis=0)
            padded = rims(jnp.concatenate([parent_stack, nest_stack], axis=0))
            parent_now = relax(padded[: line_count + 1], parent_eastward)
            nest_now = relax(padded[line_count + 1 :], nest_eastward)
        else:
            nest_now = relax(rims(nest_stack), nest_eastward)
    full_shape = (tag_count, level_count, row_count, col_count)
    return (parent_now.reshape(full_shape), nest_now.reshape(full_shape))


def deliver(parent_field, strip_tile, strip_block, strip_target, strip_count):
    tag_count, level_count, row_count, col_count = parent_field.shape
    line_count = tag_count * level_count
    block_count = row_count * col_count // 128
    tile_count, slot_total = strip_tile.shape
    own_index = lax.axis_index("tile")
    positions = jnp.arange(slot_total, dtype=jnp.int32)
    is_live = positions[None, :] < strip_count[:, None]
    from_here = jnp.logical_and(is_live, strip_tile == own_index).astype(jnp.int32)
    slot_rank = jnp.cumsum(from_here, axis=1) - 1
    slot_index = jnp.arange(CAP, dtype=jnp.int32)
    select = from_here[:, None, :] * (slot_rank[:, None, :] == slot_index[None, :, None]).astype(
        jnp.int32
    )
    source_block = jnp.sum(select * strip_block[:, None, :], axis=2).reshape(-1)
    filled = jnp.sum(select, axis=2).reshape(-1).astype(jnp.float32)
    blocks = parent_field.reshape(line_count, block_count, 128)
    packed = jnp.take(blocks, source_block, axis=1) * filled[None, :, None]
    received = lax.all_to_all(packed, "tile", split_axis=1, concat_axis=1, tiled=True)
    own_tile = lax.dynamic_index_in_dim(strip_tile, own_index, 0, keepdims=False)
    own_target = lax.dynamic_index_in_dim(strip_target, own_index, 0, keepdims=False)
    own_count = lax.dynamic_index_in_dim(strip_count, own_index, 0, keepdims=False)
    own_live = (positions < own_count).astype(jnp.int32)
    from_source = (own_tile[:, None] == jnp.arange(tile_count, dtype=jnp.int32)[None, :]).astype(
        jnp.int32
    ) * own_live[:, None]
    own_rank = jnp.sum((jnp.cumsum(from_source, axis=0) - 1) * from_source, axis=1)
    arrival = own_tile * CAP + own_rank
    pick_slot = (arrival[:, None] == jnp.arange(tile_count * CAP, dtype=jnp.int32)[None, :]).astype(
        jnp.float32
    )
    pick_slot = pick_slot * own_live[:, None].astype(jnp.float32)
    place_block = (own_target[:, None] == jnp.arange(block_count, dtype=jnp.int32)[None, :]).astype(
        jnp.float32
    )
    routing = jnp.dot(pick_slot.T, place_block, precision=HIGHEST)
    forcing = jnp.einsum("lic,ib->lbc", received, routing, precision=HIGHEST)
    return forcing.reshape(tag_count, level_count, row_count, col_count)


def shards(
    parent_field,
    nest_field,
    parent_mixing,
    parent_eastward,
    parent_northward,
    nest_eastward,
    nest_northward,
    strip_tile,
    strip_block,
    strip_target,
    strip_count,
):
    tag_count = parent_field.shape[0]
    forcing = deliver(parent_field, strip_tile, strip_block, strip_target, strip_count)
    stacked = jnp.concatenate([parent_field, parent_mixing[None]], axis=0)
    columns = lax.all_to_all(stacked, "lev", split_axis=3, concat_axis=1, tiled=True)
    column_result = tridiagonal(columns[:tag_count], columns[tag_count])
    solved = lax.all_to_all(column_result, "lev", split_axis=1, concat_axis=3, tiled=True)
    parent_adjoint, nest_adjoint = advance(
        nest_field + forcing,
        solved,
        parent_eastward,
        parent_northward,
        nest_eastward,
        nest_northward,
    )
    bulk_adjoint = lax.psum_scatter(
        jnp.sum(parent_adjoint, axis=0), "tag", scatter_dimension=2, tiled=True
    )
    return (parent_adjoint, nest_adjoint, bulk_adjoint)


def solution(mesh):
    in_specs = (
        P("tag", "lev", "tile", None),
        P("tag", "lev", "tile", None),
        P("lev", "tile", None),
        P("tile", None),
        P("tile", None),
        P("tile", None),
        P("tile", None),
        P(),
        P(),
        P(),
        P(),
    )
    out_specs = (
        P("tag", "lev", "tile", None),
        P("tag", "lev", "tile", None),
        P("lev", "tile", "tag"),
    )
    return jax.shard_map(shards, mesh=mesh, in_specs=in_specs, out_specs=out_specs, check_vma=False)
```

profile of v0, /device:TPU:2, one launch (start us, length us, event | category | flops | bytes accessed | tf_op | source)
XLA Modules:
  0.0 209.8 jit_solution(3081090923372214536)
XLA Ops:
  7.2 1.5 pad_maximum_fusion.5
  8.7 6.9 %copy.55 = f32[3,8,16,1024]{2,1,0,3:T(8,128)} copy(f32[3,8,16,1024]{3,2,1,0:T(8,128)S(1)} %pad_maximum_fusion.5) | data formatting | bytes 3145728 | tf_op jit(solution)/shard_map/concatenate | solution.py:146
  15.6 8.3 %reshape.176 = f32[4,1,98304]{2,1,0:T(1,128)} reshape(f32[1024,3,8,16]{3,2,1,0:T(8,128)} %bitcast.230) | data formatting | bytes 3145728
  23.9 5.9 %all-to-all-start = ((f32[4,1,98304]{2,1,0:T(1,128)}), f32[4,1,98304]{2,1,0:T(1,128)S(1)}, u32[]{:S(2)}, u32[]{:S(2)}) async-start(f32[4,1,98304]{2,1,0:T(1,128)} %reshape.176), calls=%async_computation | async-start | bytes 3145728 | tf_op jit(solution)/shard_map/all_to_all | solution.py:147
  29.8 1.1 reshape.159
  31.0 0.6 reduce-window.16
  32.0 0.6 select_reduce_fusion
  32.7 1.8 copy.65
  34.7 13.4 %all-to-all-done = f32[4,1,98304]{2,1,0:T(1,128)S(1)} async-done(((f32[4,1,98304]{2,1,0:T(1,128)}), f32[4,1,98304]{2,1,0:T(1,128)S(1)}, u32[]{:S(2)}, u32[]{:S(2)}) %all-to-all-start) | async-done | bytes 1572896 | tf_op jit(solution)/shard_map/all_to_all | solution.py:147
  48.1 1.2 copy-done.1
  49.2 0.5 broadcast.2764
  49.8 6.2 %reduce.4 = f32[4,98304]{1,0:T(4,128)S(1)} reduce(f32[4,1,98304]{2,1,0:T(1,128)} %copy-done.1, f32[]{:T(128)} %broadcast.2764), dimensions={1}, to_apply=%all_to_all.25.reduce_sub_computation | reduce | bytes 3145732 | tf_op jit(solution)/shard_map/all_to_all | solution.py:147
  55.9 8.9 %reshape.177 = f32[1024,3,8,16]{3,2,1,0:T(8,128)} reshape(f32[4,98304]{1,0:T(4,128)S(1)} %reduce.4) | data formatting | bytes 3145728
  64.8 7.8 %copy.69 = f32[3,8,16,4,256]{4,3,2,1,0:T(4,128)S(1)} copy(f32[3,8,16,4,256]{2,1,0,4,3:T(8,128)} %bitcast.231) | data formatting | bytes 3145728 | tf_op jit(solution)/shard_map/all_to_all | solution.py:147
  74.9 1.0 copy.59
  75.9 5.7 %all-to-all-start.1 = ((f32[2,32,16,256]{3,2,0,1:T(8,128)}), f32[2,32,16,256]{3,2,0,1:T(8,128)}, u32[]{:S(2)}, u32[]{:S(2)}) async-start(f32[2,32,16,256]{3,2,0,1:T(8,128)} %copy.59), calls=%async_computation.1 | async-start | bytes 2097152 | tf_op jit(solution)/shard_map/all_to_all | solution.py:149
  81.6 1.0 gather_fusion
  82.6 2.5 %multiply_bitcast_fusion = f32[16,256,128]{2,0,1:T(8,128)} fusion(f32[256,16,128]{2,1,0:T(8,128)S(1)} %gather_fusion, f32[256]{0:T(256)S(1)} %convert_element_type.43, pred[256]{0:T(512)(128)(4,1)S(1)} %compare_and_fusion), kind=kLoop, calls=%fused_computation.5 | loop fusion | flops 1048576 | bytes 4195584 | tf_op jit(solution)/shard_map/mul | solution.py:108
  85.2 8.3 %all-to-all-done.1 = f32[2,32,16,256]{3,2,0,1:T(8,128)} async-done(((f32[2,32,16,256]{3,2,0,1:T(8,128)}), f32[2,32,16,256]{3,2,0,1:T(8,128)}, u32[]{:S(2)}, u32[]{:S(2)}) %all-to-all-start.1) | async-done | bytes 1048608 | tf_op jit(solution)/shard_map/all_to_all | solution.py:149
  93.4 9.6 %all-to-all-start.2 = ((f32[16,256,128]{2,0,1:T(8,128)}), f32[16,256,128]{2,0,1:T(8,128)}, u32[]{:S(2)}, u32[]{:S(2)}) async-start(f32[16,256,128]{2,0,1:T(8,128)} %multiply_bitcast_fusion), calls=%async_computation.2 | async-start | bytes 4194304 | tf_op jit(solution)/shard_map/all_to_all | solution.py:109
  103.1 0.6 dynamic_slice.12
  103.7 0.7 compare_convert_fusion.1
  104.3 0.7 constant_dynamic-slice_fusion
  105.1 0.6 reduce-window.14
  106.0 0.7 compare_convert_fusion
  106.7 0.7 fusion.86
  107.9 1.9 copy.61
  109.8 0.5 reshape.154
  110.4 1.7 fusion.137
  112.1 40.2 %all-to-all-done.2 = f32[16,256,128]{2,0,1:T(8,128)} async-done(((f32[16,256,128]{2,0,1:T(8,128)}), f32[16,256,128]{2,0,1:T(8,128)}, u32[]{:S(2)}, u32[]{:S(2)}) %all-to-all-start.2) | async-done | bytes 2097184 | tf_op jit(solution)/shard_map/all_to_all | solution.py:109
  152.3 3.4 %fusion.4 = f32[16,128,128]{2,1,0:T(8,128)S(1)} fusion(f32[256,128,1]{0,1,2:T(8,128)S(1)} %convolution_bitcast_fusion, f32[16,256,128]{2,0,1:T(8,128)} %all-to-all-done.2), kind=kOutput, calls=%fused_computation.12 | convolution fusion | flops 805306368 | bytes 3276800 | tf_op jit(solution)/shard_map/lic,ib->lbc/dot_general | solution.py:127
  155.9 1.4 add.2442
  157.5 2.1 collective-permute-start.1
  159.6 1.3 collective-permute-start
  161.3 1.5 collective-permute-done
  162.9 0.7 fusion.13
  163.6 1.7 fusion.135
  165.4 5.2 %collective-permute-start.3 = (f32[17,1,1024]{2,1,0:T(1,128)S(1)}, f32[17,1,1024]{2,1,0:T(1,128)S(1)}, u32[]{:S(2)}, u32[]{:S(2)}) collective-permute-start(f32[17,1,1024]{2,1,0:T(1,128)S(1)} %get-tuple-element.88), channel_id=1, source_target_pairs={{0,16},{16,32},{32,48},{48,64},{64,80},{80,96},{96,112},{112,128},... | collective-permute-start | bytes 208904 | tf_op jit(solution)/shard_map/ppermute | solution.py:19
  170.7 1.5 collective-permute-start.2
  172.2 1.7 fusion.35
  173.9 2.1 %reduce_sum.39 = f32[8,16,1024]{2,1,0:T(8,128)} reduce(f32[2,8,16,1024]{3,2,1,0:T(8,128)} %bitcast.265, f32[]{:T(128)} %constant.48.clone.1), dimensions={0}, to_apply=%region_7.8 | reduce | flops 131072 | bytes 1572868 | tf_op jit(solution)/shard_map/reduce_sum | solution.py:159
  176.4 0.9 copy-done.3
  177.6 0.6 fusion.20
  178.4 3.0 %collective-permute-start.5 = (f32[17,1,1024]{2,1,0:T(1,128)S(1)}, f32[17,1,1024]{2,1,0:T(1,128)S(1)}, u32[]{:S(2)}, u32[]{:S(2)}) collective-permute-start(f32[17,1,1024]{2,1,0:T(1,128)S(1)} %get-tuple-element.86), channel_id=1, source_target_pairs={{0,16},{16,32},{32,48},{48,64},{64,80},{80,96},{96,112},{112,128},... | collective-permute-start | bytes 208904 | tf_op jit(solution)/shard_map/ppermute | solution.py:19
  181.8 1.3 collective-permute-start.4
  183.4 2.3 %collective-permute-done.4 = f32[17,1,1024]{2,1,0:T(1,128)S(1)} collective-permute-done((f32[17,1,1024]{2,1,0:T(1,128)S(1)}, f32[17,1,1024]{2,1,0:T(1,128)S(1)}, u32[]{:S(2)}, u32[]{:S(2)}) %collective-permute-start.4) | collective-permute-done | bytes 69664 | tf_op jit(solution)/shard_map/ppermute | solution.py:21
  185.7 1.6 fusion.27
  187.3 15.6 %reduce-scatter.2.cloned.1.call-done = f32[8,16,256]{2,1,0:T(8,128)} async-done(((f32[8,16,1024]{2,1,0:T(8,128)}), f32[8,16,256]{2,1,0:T(8,128)}) %reduce-scatter.2.cloned.1.call-update) | async-done | bytes 131088 | tf_op jit(solution)/shard_map/reduce_scatter | solution.py:158
  (118 shorter events, 5.8 us)
Async XLA Ops:
  23.9 5.9 %copy-start.2 = (f32[2,8,16,1024]{3,2,1,0:T(8,128)S(1)}, f32[2,8,16,1024]{3,2,1,0:T(8,128)}, u32[]{:S(2)}) copy-start(f32[2,8,16,1024]{3,2,1,0:T(8,128)} %param.11) | copy-start | bytes 3145732
  23.9 24.2 %all-to-all-start = ((f32[4,1,98304]{2,1,0:T(1,128)}), f32[4,1,98304]{2,1,0:T(1,128)S(1)}, u32[]{:S(2)}, u32[]{:S(2)}) async-start(f32[4,1,98304]{2,1,0:T(1,128)} %reshape.176), calls=%async_computation | async-start | bytes 3145728 | tf_op jit(solution)/shard_map/all_to_all | solution.py:147
  29.8 1.1 copy-start.10
  29.8 1.1 copy-start.12
  29.8 2.2 %copy-start.11 = (s32[16,256]{1,0:T(8,128)S(1)}, s32[16,256]{1,0:T(8,128)}, u32[]{:S(2)}) copy-start(s32[16,256]{1,0:T(8,128)} %param.19) | copy-start | bytes 49156
  48.1 1.2 copy-start.1
  75.9 17.5 %all-to-all-start.1 = ((f32[2,32,16,256]{3,2,0,1:T(8,128)}), f32[2,32,16,256]{3,2,0,1:T(8,128)}, u32[]{:S(2)}, u32[]{:S(2)}) async-start(f32[2,32,16,256]{3,2,0,1:T(8,128)} %copy.59), calls=%async_computation.1 | async-start | bytes 2097152 | tf_op jit(solution)/shard_map/all_to_all | solution.py:149
  85.2 20.7 %copy-start.8 = (f32[16,1024]{1,0:T(8,128)S(1)}, f32[16,1024]{1,0:T(8,128)}, u32[]{:S(2)}) copy-start(f32[16,1024]{1,0:T(8,128)} %param.16) | copy-start | bytes 196612
  85.2 20.8 %copy-start.9 = (f32[16,1024]{1,0:T(8,128)S(1)}, f32[16,1024]{1,0:T(8,128)}, u32[]{:S(2)}) copy-start(f32[16,1024]{1,0:T(8,128)} %param.14) | copy-start | bytes 196612
  93.4 58.9 %all-to-all-start.2 = ((f32[16,256,128]{2,0,1:T(8,128)}), f32[16,256,128]{2,0,1:T(8,128)}, u32[]{:S(2)}, u32[]{:S(2)}) async-start(f32[16,256,128]{2,0,1:T(8,128)} %multiply_bitcast_fusion), calls=%async_computation.2 | async-start | bytes 4194304 | tf_op jit(solution)/shard_map/all_to_all | solution.py:109
  103.0 99.9 %reduce-scatter.2.cloned.1.call-start = ((), (), s32[]{:S(2)}) async-start(), calls=%async_computation.4 | async-start | bytes 655360 | tf_op jit(solution)/shard_map/reduce_scatter | solution.py:158
  155.8 1.4 copy-start
  155.8 1.4 copy-start.7
  157.5 3.8 %collective-permute-start.1 = (f32[34,1,1024]{2,1,0:T(1,128)S(1)}, f32[34,1,1024]{2,1,0:T(1,128)S(1)}, u32[]{:S(2)}, u32[]{:S(2)}) collective-permute-start(f32[34,1,1024]{2,1,0:T(1,128)S(1)} %get-tuple-element.84), channel_id=1, source_target_pairs={{0,16},{16,32},{32,48},{48,64},{64,80},{80,96},{96,112},{112,128},... | collective-permute-start | bytes 417800 | tf_op jit(solution)/shard_map/ppermute | solution.py:19
  159.6 3.3 %collective-permute-start = (f32[34,1,1024]{2,1,0:T(1,128)S(1)}, f32[34,1,1024]{2,1,0:T(1,128)S(1)}, u32[]{:S(2)}, u32[]{:S(2)}) collective-permute-start(f32[34,1,1024]{2,1,0:T(1,128)S(1)} %get-tuple-element.83), channel_id=1, source_target_pairs={{16,0},{32,16},{48,32},{64,48},{80,64},{96,80},{112,96},{128,112},... | collective-permute-start | bytes 417800 | tf_op jit(solution)/shard_map/ppermute | solution.py:21
  163.6 8.6 %copy-start.6 = (f32[16,16,1023]{2,1,0:T(8,128)S(1)}, f32[16,16,1023]{2,1,0:T(8,128)}, u32[]{:S(2)}) copy-start(f32[16,16,1023]{2,1,0:T(8,128)} %get-tuple-element.96) | copy-start | bytes 3142660
  165.3 6.9 %copy-start.5 = (f32[16,16,1023]{2,1,0:T(8,128)S(1)}, f32[16,16,1023]{2,1,0:T(8,128)}, u32[]{:S(2)}) copy-start(f32[16,16,1023]{2,1,0:T(8,128)} %get-tuple-element.95) | copy-start | bytes 3142660
  165.4 10.7 %collective-permute-start.3 = (f32[17,1,1024]{2,1,0:T(1,128)S(1)}, f32[17,1,1024]{2,1,0:T(1,128)S(1)}, u32[]{:S(2)}, u32[]{:S(2)}) collective-permute-start(f32[17,1,1024]{2,1,0:T(1,128)S(1)} %get-tuple-element.88), channel_id=1, source_target_pairs={{0,16},{16,32},{32,48},{48,64},{64,80},{80,96},{96,112},{112,128},... | collective-permute-start | bytes 208904 | tf_op jit(solution)/shard_map/ppermute | solution.py:19
  170.7 5.7 %collective-permute-start.2 = (f32[17,1,1024]{2,1,0:T(1,128)S(1)}, f32[17,1,1024]{2,1,0:T(1,128)S(1)}, u32[]{:S(2)}, u32[]{:S(2)}) collective-permute-start(f32[17,1,1024]{2,1,0:T(1,128)S(1)} %get-tuple-element.87), channel_id=1, source_target_pairs={{16,0},{32,16},{48,32},{64,48},{80,64},{96,80},{112,96},{128,112},... | collective-permute-start | bytes 208904 | tf_op jit(solution)/shard_map/ppermute | solution.py:21
  176.1 1.2 copy-start.3
  176.1 1.5 copy-start.4
  178.4 4.7 %collective-permute-start.5 = (f32[17,1,1024]{2,1,0:T(1,128)S(1)}, f32[17,1,1024]{2,1,0:T(1,128)S(1)}, u32[]{:S(2)}, u32[]{:S(2)}) collective-permute-start(f32[17,1,1024]{2,1,0:T(1,128)S(1)} %get-tuple-element.86), channel_id=1, source_target_pairs={{0,16},{16,32},{32,48},{48,64},{64,80},{80,96},{96,112},{112,128},... | collective-permute-start | bytes 208904 | tf_op jit(solution)/shard_map/ppermute | solution.py:19
  181.8 3.9 %collective-permute-start.4 = (f32[17,1,1024]{2,1,0:T(1,128)S(1)}, f32[17,1,1024]{2,1,0:T(1,128)S(1)}, u32[]{:S(2)}, u32[]{:S(2)}) collective-permute-start(f32[17,1,1024]{2,1,0:T(1,128)S(1)} %get-tuple-element.85), channel_id=1, source_target_pairs={{16,0},{32,16},{48,32},{64,48},{80,64},{96,80},{112,96},{128,112},... | collective-permute-start | bytes 208904 | tf_op jit(solution)/shard_map/ppermute | solution.py:21
Sparse Core Ops, SparseCore 0:
  176.2 26.7 reduce-scatter.1
where the time goes:
time: 211 us; the launch traced here: 210 us
  waiting for transfers between devices  81.3 us (39%)
  local copies, waits for them, and re-layouts  49.5 us (23%)
  starting transfers between devices  35.7 us (17%)
  other arithmetic  24.7 us (12%)
  between operations  14.8 us (7%)
  matrix products  3.79 us (2%)
    all_to_all x1, waiting for transfers between devices, deliver(): lax.all_to_all(packed, 'tile', split_axis=1, concat_axis=1, tiled=True)  40.2 us
    unnamed x43, local copies, waits for them, and re-layouts  19.7 us
    reduce_scatter x1, waiting for transfers between devices, shards(): lax.psum_scatter(jnp.sum(parent_adjoint, axis=0), 'tag', scatter_dimensio...  15.6 us
    all_to_all x1, waiting for transfers between devices, shards(): lax.all_to_all(stacked, 'lev', split_axis=3, concat_axis=1, tiled=True)  13.4 us
    ppermute x3, starting transfers between devices, extended(): lax.ppermute(tail, axis, [(i, (i + 1) % count) for i in range(ends)])  10.3 us
    all_to_all x1, starting transfers between devices, deliver(): lax.all_to_all(packed, 'tile', split_axis=1, concat_axis=1, tiled=True)  9.61 us
    all_to_all x2, local copies, waits for them, and re-layouts, shards(): lax.all_to_all(stacked, 'lev', split_axis=3, concat_axis=1, tiled=True)  8.35 us
    all_to_all x1, waiting for transfers between devices, shards(): lax.all_to_all(column_result, 'lev', split_axis=1, concat_axis=3, tiled=T...  8.27 us
  transfers between devices with their start and end apart: 10, of which 6 were waited for; matrix products, arithmetic and copies ran while one was open for 12% of the time, Pallas kernels for 0%

commit v1 on v0

--- a/solution.py
+++ b/solution.py
@@ -144,7 +144,11 @@
     tag_count = parent_field.shape[0]
     forcing = deliver(parent_field, strip_tile, strip_block, strip_target, strip_count)
     stacked = jnp.concatenate([parent_field, parent_mixing[None]], axis=0)
-    columns = lax.all_to_all(stacked, "lev", split_axis=3, concat_axis=1, tiled=True)
+    then = lax.axis_size("lev")
+    raw_out = jnp.split(stacked, then, 3)
+    y1 = jnp.stack(raw_out, axis=0)
+    later = lax.all_to_all(y1, "lev", 0, 0)
+    columns = jnp.concatenate(later, 1)
     column_result = tridiagonal(columns[:tag_count], columns[tag_count])
     solved = lax.all_to_all(column_result, "lev", split_axis=1, concat_axis=3, tiled=True)
     parent_adjoint, nest_adjoint = advance(

time: 211 us -> 172 us (0.82)
  local copies, waits for them, and re-layouts: 49.5 us -> 15.5 us
  other arithmetic: 24.7 us -> 19.9 us
    unnamed x43 -> x39, local copies, waits for them, and re-layouts: 19.7 us -> 1.35 us
    all_to_all x2 -> x1, local copies, waits for them, and re-layouts: 8.35 us -> 0.12 us  [shards(): later = lax.all_to_all(y1, 'lev', 0, 0)]
    concatenate x1 -> x0, local copies, waits for them, and re-layouts: 6.92 us -> none  [shards(): stacked = jnp.concatenate([parent_field, parent_mixing[None]], axis=0)]
    all_to_all x1 -> x0, other arithmetic: 6.16 us -> none  [shards(): lax.all_to_all(stacked, 'lev', split_axis=3, concat_axis=1, tiled=True)]
    another operation x5 -> x7, other arithmetic: 1.3 us -> 4.15 us  [the longest x2 2.85 us: shards(): y1 = jnp.stack(raw_out, axis=0)]
  transfers between devices with their start and end apart: 10 -> 10, of which waited for: 6 -> 6; matrix products, arithmetic and copies ran while one was open for 12% -> 15% of each run, Pallas kernels for 0% -> 0%
where the time goes in v1:
time: 172 us; the launch traced here: 171 us
  waiting for transfers between devices  81.4 us (47%)
  starting transfers between devices  35.5 us (21%)
  other arithmetic  19.9 us (12%)
  local copies, waits for them, and re-layouts  15.5 us (9%)
  between operations  14.7 us (9%)
  matrix products  3.78 us (2%)
    all_to_all x1, waiting for transfers between devices, deliver(): lax.all_to_all(packed, 'tile', split_axis=1, concat_axis=1, tiled=True)  40.2 us
    reduce_scatter x1, waiting for transfers between devices, shards(): lax.psum_scatter(jnp.sum(parent_adjoint, axis=0), 'tag', scatter_dimensio...  15.6 us
    all_to_all x1, waiting for transfers between devices, shards(): later = lax.all_to_all(y1, 'lev', 0, 0)  13.4 us
    ppermute x3, starting transfers between devices, extended(): lax.ppermute(tail, axis, [(i, (i + 1) % count) for i in range(ends)])  10.4 us
    all_to_all x1, starting transfers between devices, deliver(): lax.all_to_all(packed, 'tile', split_axis=1, concat_axis=1, tiled=True)  9.61 us
    all_to_all x1, waiting for transfers between devices, shards(): lax.all_to_all(column_result, 'lev', split_axis=1, concat_axis=3, tiled=T...  8.3 us
    all_to_all x1, starting transfers between devices, shards(): later = lax.all_to_all(y1, 'lev', 0, 0)  5.93 us
    all_to_all x1, starting transfers between devices, shards(): lax.all_to_all(column_result, 'lev', split_axis=1, concat_axis=3, tiled=T...  5.67 us
  transfers between devices with their start and end apart: 10, of which 6 were waited for; matrix products, arithmetic and copies ran while one was open for 15% of the time, Pallas kernels for 0%

profile of v1, /device:TPU:2, one launch (start us, length us, event | category | flops | bytes accessed | tf_op | source)
XLA Modules:
  0.0 170.8 jit_solution(6059116242555972395)
XLA Ops:
  7.2 1.5 fusion.41
  8.7 1.3 pad_maximum_fusion.5
  10.0 5.9 %all-to-all-start = ((f32[4,3,8,16,256]{4,3,2,1,0:T(8,128)}), f32[4,3,8,16,256]{4,3,2,1,0:T(8,128)S(1)}, u32[]{:S(2)}, u32[]{:S(2)}) async-start(f32[4,3,8,16,256]{4,3,2,1,0:T(8,128)} %pad_maximum_fusion.5), calls=%async_computation | async-start | bytes 3145728 | tf_op jit(solution)/shard_map/all_to_all | solution.py:150
  16.0 1.1 reshape.164
  17.2 0.6 reduce-window.16
  18.1 0.6 select_reduce_fusion
  18.9 1.8 %copy.49 = f32[16,128,128]{2,0,1:T(8,128)S(1)} copy(f32[16,128,128]{2,1,0:T(8,128)} %reshape.164) | data formatting | bytes 2097152 | tf_op jit(solution)/shard_map/reshape | solution.py:107
  20.8 13.4 %all-to-all-done = f32[4,3,8,16,256]{4,3,2,1,0:T(8,128)S(1)} async-done(((f32[4,3,8,16,256]{4,3,2,1,0:T(8,128)}), f32[4,3,8,16,256]{4,3,2,1,0:T(8,128)S(1)}, u32[]{:S(2)}, u32[]{:S(2)}) %all-to-all-start) | async-done | bytes 1572896 | tf_op jit(solution)/shard_map/all_to_all | solution.py:150
  35.2 0.4 constant_dynamic-update-slice_fusion.31
  36.0 1.0 copy.43
  37.1 5.7 %all-to-all-start.1 = ((f32[2,32,16,256]{3,2,0,1:T(8,128)}), f32[2,32,16,256]{3,2,0,1:T(8,128)}, u32[]{:S(2)}, u32[]{:S(2)}) async-start(f32[2,32,16,256]{3,2,0,1:T(8,128)} %copy.43), calls=%async_computation.1 | async-start | bytes 2097152 | tf_op jit(solution)/shard_map/all_to_all | solution.py:153
  42.7 1.0 gather_fusion
  43.8 2.5 %multiply_bitcast_fusion = f32[16,256,128]{2,0,1:T(8,128)} fusion(f32[256,16,128]{2,1,0:T(8,128)S(1)} %gather_fusion, f32[256]{0:T(256)S(1)} %convert_element_type.43, pred[256]{0:T(512)(128)(4,1)S(1)} %compare_and_fusion), kind=kLoop, calls=%fused_computation.8 | loop fusion | flops 1048576 | bytes 4195584 | tf_op jit(solution)/shard_map/mul | solution.py:108
  46.3 8.3 %all-to-all-done.1 = f32[2,32,16,256]{3,2,0,1:T(8,128)} async-done(((f32[2,32,16,256]{3,2,0,1:T(8,128)}), f32[2,32,16,256]{3,2,0,1:T(8,128)}, u32[]{:S(2)}, u32[]{:S(2)}) %all-to-all-start.1) | async-done | bytes 1048608 | tf_op jit(solution)/shard_map/all_to_all | solution.py:153
  54.6 9.6 %all-to-all-start.2 = ((f32[16,256,128]{2,0,1:T(8,128)}), f32[16,256,128]{2,0,1:T(8,128)}, u32[]{:S(2)}, u32[]{:S(2)}) async-start(f32[16,256,128]{2,0,1:T(8,128)} %multiply_bitcast_fusion), calls=%async_computation.2 | async-start | bytes 4194304 | tf_op jit(solution)/shard_map/all_to_all | solution.py:109
  64.3 0.6 dynamic_slice.12
  64.8 0.7 compare_convert_fusion.1
  65.5 0.7 constant_dynamic-slice_fusion
  66.2 0.6 reduce-window.14
  67.2 0.7 fusion.93
  67.9 0.7 compare_convert_fusion
  68.6 0.4 convolution_bitcast_fusion
  69.0 1.9 %copy.45 = f32[2,8,16,4,256]{4,3,2,1,0:T(4,128)S(1)} copy(f32[2,8,16,4,256]{4,2,0,1,3:T(8,128)} %bitcast.105) | data formatting | bytes 2097152 | tf_op jit(solution)/shard_map/all_to_all | solution.py:153
  71.0 0.5 reshape.159
  71.5 1.7 fusion.144
  73.2 40.2 %all-to-all-done.2 = f32[16,256,128]{2,0,1:T(8,128)} async-done(((f32[16,256,128]{2,0,1:T(8,128)}), f32[16,256,128]{2,0,1:T(8,128)}, u32[]{:S(2)}, u32[]{:S(2)}) %all-to-all-start.2) | async-done | bytes 2097184 | tf_op jit(solution)/shard_map/all_to_all | solution.py:109
  113.4 3.4 %fusion.4 = f32[16,128,128]{2,1,0:T(8,128)S(1)} fusion(f32[256,128,1]{0,1,2:T(8,128)S(1)} %convolution_bitcast_fusion, f32[16,256,128]{2,0,1:T(8,128)} %all-to-all-done.2), kind=kOutput, calls=%fused_computation.19 | convolution fusion | flops 805306368 | bytes 3276800 | tf_op jit(solution)/shard_map/lic,ib->lbc/dot_general | solution.py:127
  117.0 1.4 add.2442
  118.7 2.1 %collective-permute-start.1 = (f32[34,1,1024]{2,1,0:T(1,128)S(1)}, f32[34,1,1024]{2,1,0:T(1,128)S(1)}, u32[]{:S(2)}, u32[]{:S(2)}) collective-permute-start(f32[34,1,1024]{2,1,0:T(1,128)S(1)} %get-tuple-element.84), channel_id=1, source_target_pairs={{0,16},{16,32},{32,48},{48,64},{64,80},{80,96},{96,112},{112,128},... | collective-permute-start | bytes 417800 | tf_op jit(solution)/shard_map/ppermute | solution.py:19
  120.8 1.3 collective-permute-start
  122.1 0.4 fusion.143
  122.5 1.5 collective-permute-done
  124.0 0.7 fusion.13
  124.9 1.7 fusion.142
  126.6 5.3 %collective-permute-start.3 = (f32[17,1,1024]{2,1,0:T(1,128)S(1)}, f32[17,1,1024]{2,1,0:T(1,128)S(1)}, u32[]{:S(2)}, u32[]{:S(2)}) collective-permute-start(f32[17,1,1024]{2,1,0:T(1,128)S(1)} %get-tuple-element.92), channel_id=1, source_target_pairs={{0,16},{16,32},{32,48},{48,64},{64,80},{80,96},{96,112},{112,128},... | collective-permute-start | bytes 208904 | tf_op jit(solution)/shard_map/ppermute | solution.py:19
  131.9 1.3 collective-permute-start.2
  133.2 1.7 %fusion.35 = f32[16,16,1024]{2,1,0:T(8,128)} fusion(f32[16,16,1024]{2,1,0:T(8,128)S(1)} %reshape.159, f32[34,1,1024]{2,1,0:T(1,128)S(1)} %collective-permute-done.1, f32[1,16,1024]{2,1,0:T(8,128)S(1)} %bitcast.259, f32[16,16,1024]{2,1,0:T(8,128)S(1)} %bitcast.236, f32[1,16,1024]{2,1,0:T(8,128)S(1)} %bitcast.275, f32[34,1,1024]{2,1,0:T(1,128)S(1)} %collective-permute-done, ...), kind=kLoop, calls=%fused_computation.61 | loop fusion | flops 5242880 | bytes 5912576 | tf_op jit(solution)/shard_map/add | solution.py:61
  134.9 2.1 %reduce_sum.39 = f32[8,16,1024]{2,1,0:T(8,128)} reduce(f32[2,8,16,1024]{3,2,1,0:T(8,128)} %bitcast.270, f32[]{:T(128)} %constant.48.clone.1), dimensions={0}, to_apply=%region_7.8 | reduce | flops 131072 | bytes 1572868 | tf_op jit(solution)/shard_map/reduce_sum | solution.py:163
  137.4 0.9 copy-done.2
  138.3 0.3 copy-done.3
  138.6 0.6 fusion.20
  139.3 3.0 %collective-permute-start.5 = (f32[17,1,1024]{2,1,0:T(1,128)S(1)}, f32[17,1,1024]{2,1,0:T(1,128)S(1)}, u32[]{:S(2)}, u32[]{:S(2)}) collective-permute-start(f32[17,1,1024]{2,1,0:T(1,128)S(1)} %get-tuple-element.90), channel_id=1, source_target_pairs={{0,16},{16,32},{32,48},{48,64},{64,80},{80,96},{96,112},{112,128},... | collective-permute-start | bytes 208904 | tf_op jit(solution)/shard_map/ppermute | solution.py:19
  142.4 0.4 fusion.141
  142.8 1.3 collective-permute-start.4
  144.1 0.3 fusion.3
  144.4 2.3 %collective-permute-done.4 = f32[17,1,1024]{2,1,0:T(1,128)S(1)} collective-permute-done((f32[17,1,1024]{2,1,0:T(1,128)S(1)}, f32[17,1,1024]{2,1,0:T(1,128)S(1)}, u32[]{:S(2)}, u32[]{:S(2)}) %collective-permute-start.4) | collective-permute-done | bytes 69664 | tf_op jit(solution)/shard_map/ppermute | solution.py:21
  146.7 1.6 fusion.27
  148.3 15.6 %reduce-scatter.2.cloned.1.call-done = f32[8,16,256]{2,1,0:T(8,128)} async-done(((f32[8,16,1024]{2,1,0:T(8,128)}), f32[8,16,256]{2,1,0:T(8,128)}) %reduce-scatter.2.cloned.1.call-update) | async-done | bytes 131088 | tf_op jit(solution)/shard_map/reduce_scatter | solution.py:162
  (110 shorter events, 3.3 us)
Async XLA Ops:
  10.0 5.9 %copy-start.1 = (f32[2,8,16,1024]{3,2,1,0:T(8,128)S(1)}, f32[2,8,16,1024]{3,2,1,0:T(8,128)}, u32[]{:S(2)}) copy-start(f32[2,8,16,1024]{3,2,1,0:T(8,128)} %param.11) | copy-start | bytes 3145732
  10.0 24.2 %all-to-all-start = ((f32[4,3,8,16,256]{4,3,2,1,0:T(8,128)}), f32[4,3,8,16,256]{4,3,2,1,0:T(8,128)S(1)}, u32[]{:S(2)}, u32[]{:S(2)}) async-start(f32[4,3,8,16,256]{4,3,2,1,0:T(8,128)} %pad_maximum_fusion.5), calls=%async_computation | async-start | bytes 3145728 | tf_op jit(solution)/shard_map/all_to_all | solution.py:150
  16.0 1.1 copy-start.9
  16.0 1.1 copy-start.11
  16.0 2.2 %copy-start.10 = (s32[16,256]{1,0:T(8,128)S(1)}, s32[16,256]{1,0:T(8,128)}, u32[]{:S(2)}) copy-start(s32[16,256]{1,0:T(8,128)} %param.19) | copy-start | bytes 49156
  37.1 17.5 %all-to-all-start.1 = ((f32[2,32,16,256]{3,2,0,1:T(8,128)}), f32[2,32,16,256]{3,2,0,1:T(8,128)}, u32[]{:S(2)}, u32[]{:S(2)}) async-start(f32[2,32,16,256]{3,2,0,1:T(8,128)} %copy.43), calls=%async_computation.1 | async-start | bytes 2097152 | tf_op jit(solution)/shard_map/all_to_all | solution.py:153
  46.3 20.8 %copy-start.8 = (f32[16,1024]{1,0:T(8,128)S(1)}, f32[16,1024]{1,0:T(8,128)}, u32[]{:S(2)}) copy-start(f32[16,1024]{1,0:T(8,128)} %param.14) | copy-start | bytes 196612
  46.3 20.8 %copy-start.7 = (f32[16,1024]{1,0:T(8,128)S(1)}, f32[16,1024]{1,0:T(8,128)}, u32[]{:S(2)}) copy-start(f32[16,1024]{1,0:T(8,128)} %param.16) | copy-start | bytes 196612
  54.6 58.9 %all-to-all-start.2 = ((f32[16,256,128]{2,0,1:T(8,128)}), f32[16,256,128]{2,0,1:T(8,128)}, u32[]{:S(2)}, u32[]{:S(2)}) async-start(f32[16,256,128]{2,0,1:T(8,128)} %multiply_bitcast_fusion), calls=%async_computation.2 | async-start | bytes 4194304 | tf_op jit(solution)/shard_map/all_to_all | solution.py:109
  64.2 99.7 %reduce-scatter.2.cloned.1.call-start = ((), (), s32[]{:S(2)}) async-start(), calls=%async_computation.4 | async-start | bytes 655360 | tf_op jit(solution)/shard_map/reduce_scatter | solution.py:162
  117.0 1.4 copy-start
  117.0 1.4 copy-start.6
  118.7 3.8 %collective-permute-start.1 = (f32[34,1,1024]{2,1,0:T(1,128)S(1)}, f32[34,1,1024]{2,1,0:T(1,128)S(1)}, u32[]{:S(2)}, u32[]{:S(2)}) collective-permute-start(f32[34,1,1024]{2,1,0:T(1,128)S(1)} %get-tuple-element.84), channel_id=1, source_target_pairs={{0,16},{16,32},{32,48},{48,64},{64,80},{80,96},{96,112},{112,128},... | collective-permute-start | bytes 417800 | tf_op jit(solution)/shard_map/ppermute | solution.py:19
  120.8 3.3 %collective-permute-start = (f32[34,1,1024]{2,1,0:T(1,128)S(1)}, f32[34,1,1024]{2,1,0:T(1,128)S(1)}, u32[]{:S(2)}, u32[]{:S(2)}) collective-permute-start(f32[34,1,1024]{2,1,0:T(1,128)S(1)} %get-tuple-element.83), channel_id=1, source_target_pairs={{16,0},{32,16},{48,32},{64,48},{80,64},{96,80},{112,96},{128,112},... | collective-permute-start | bytes 417800 | tf_op jit(solution)/shard_map/ppermute | solution.py:21
  124.9 8.3 %copy-start.4 = (f32[16,16,1023]{2,1,0:T(8,128)S(1)}, f32[16,16,1023]{2,1,0:T(8,128)}, u32[]{:S(2)}) copy-start(f32[16,16,1023]{2,1,0:T(8,128)} %get-tuple-element.99) | copy-start | bytes 3142660
  124.9 8.3 %copy-start.5 = (f32[16,16,1023]{2,1,0:T(8,128)S(1)}, f32[16,16,1023]{2,1,0:T(8,128)}, u32[]{:S(2)}) copy-start(f32[16,16,1023]{2,1,0:T(8,128)} %get-tuple-element.100) | copy-start | bytes 3142660
  126.6 10.5 %collective-permute-start.3 = (f32[17,1,1024]{2,1,0:T(1,128)S(1)}, f32[17,1,1024]{2,1,0:T(1,128)S(1)}, u32[]{:S(2)}, u32[]{:S(2)}) collective-permute-start(f32[17,1,1024]{2,1,0:T(1,128)S(1)} %get-tuple-element.92), channel_id=1, source_target_pairs={{0,16},{16,32},{32,48},{48,64},{64,80},{80,96},{96,112},{112,128},... | collective-permute-start | bytes 208904 | tf_op jit(solution)/shard_map/ppermute | solution.py:19
  131.9 5.5 %collective-permute-start.2 = (f32[17,1,1024]{2,1,0:T(1,128)S(1)}, f32[17,1,1024]{2,1,0:T(1,128)S(1)}, u32[]{:S(2)}, u32[]{:S(2)}) collective-permute-start(f32[17,1,1024]{2,1,0:T(1,128)S(1)} %get-tuple-element.91), channel_id=1, source_target_pairs={{16,0},{32,16},{48,32},{64,48},{80,64},{96,80},{112,96},{128,112},... | collective-permute-start | bytes 208904 | tf_op jit(solution)/shard_map/ppermute | solution.py:21
  137.0 1.2 copy-start.2
  137.1 1.5 copy-start.3
  139.3 4.7 %collective-permute-start.5 = (f32[17,1,1024]{2,1,0:T(1,128)S(1)}, f32[17,1,1024]{2,1,0:T(1,128)S(1)}, u32[]{:S(2)}, u32[]{:S(2)}) collective-permute-start(f32[17,1,1024]{2,1,0:T(1,128)S(1)} %get-tuple-element.90), channel_id=1, source_target_pairs={{0,16},{16,32},{32,48},{48,64},{64,80},{80,96},{96,112},{112,128},... | collective-permute-start | bytes 208904 | tf_op jit(solution)/shard_map/ppermute | solution.py:19
  142.8 3.9 %collective-permute-start.4 = (f32[17,1,1024]{2,1,0:T(1,128)S(1)}, f32[17,1,1024]{2,1,0:T(1,128)S(1)}, u32[]{:S(2)}, u32[]{:S(2)}) collective-permute-start(f32[17,1,1024]{2,1,0:T(1,128)S(1)} %get-tuple-element.89), channel_id=1, source_target_pairs={{16,0},{32,16},{48,32},{64,48},{80,64},{96,80},{112,96},{128,112},... | collective-permute-start | bytes 208904 | tf_op jit(solution)/shard_map/ppermute | solution.py:21
Sparse Core Ops, SparseCore 0:
  137.2 26.7 reduce-scatter.1
